TPU v7x, 32 devices: a whole 2x2x4 slice. The times are simulated.
32 devices in a mesh: expert: 4 (over y, x), blk: 8 (over z, core).
Axes of the slice: x: 2, y: 2, z: 4, core: 2. Of those that a mesh axis runs over, the one named last changes fastest.
Arguments:
- tokens: bfloat16 [512, 3072], P('expert', 'blk'), may hold values from -6 to 6
- routes: int32 [512, 2], P('expert'), may hold values from 0 to 3, all different within a row; in each aligned block of 128 rows (0 to 127, 128 to 255, ...) at most 128 rows name the same one
- labels: int32 [512], P('expert'), may hold values from 0 to 15
- gate_weight: bfloat16 [4, 3072, 8192], P('expert', None, 'blk'), may hold values from -0.109375 to 0.109375
- up_weight: bfloat16 [4, 3072, 8192], P('expert', None, 'blk'), may hold values from -0.109375 to 0.109375
Outputs:
- moment: bfloat16 [4, 8192, 8192], P('expert', 'blk')
- cross_moment: float32 [4, 8192, 16], P('expert', 'blk')
Inputs may be any that keep to these rules, and one draw needn't show every extreme that they name: `routes`: in the rows of one token shard (128 rows), no expert is named by more than 128 rows, and in some shard one expert is named by exactly 128 rows; every expert is named by some row; a row names 2 different experts.
All inputs are finite; a program needn't handle non-finite values.
Results may differ from a plain program's by a relative error of at most 0.0057.
Values may be sent and summed in bfloat16 or wider, within the bound.
A program may use at most 128 MiB of HBM per device.

v0:
```python
import jax
import jax.numpy as jnp
from jax import lax
from jax.sharding import PartitionSpec as P

CLASSES = 16


def shards(tokens, routes, labels, gate_weight, up_weight):
    groups = lax.axis_size("expert")
    tok_rows = tokens.shape[0]
    top_count = routes.shape[1]
    slot_count = min(tok_rows, 2 * tok_rows * top_count // groups)
    targets = jnp.arange(groups, dtype=jnp.int32)
    hit_mask = jnp.any(routes[:, :, None] == targets[None, None, :], axis=1).astype(jnp.int32)
    rank_pos = jnp.cumsum(hit_mask, axis=0) - hit_mask
    places = jnp.arange(slot_count, dtype=jnp.int32)
    selector = (hit_mask.T[:, None, :] > 0) & (rank_pos.T[:, None, :] == places[None, :, None])
    tag_out = jnp.sum(jnp.where(selector, labels[None, None, :] + 1, 0), axis=2)
    select_mat = selector.astype(jnp.bfloat16)
    arrived = lax.all_to_all(
        jnp.einsum("est,td->esd", select_mat, tokens, preferred_element_type=jnp.float32).astype(
            jnp.bfloat16
        ),
        "expert",
        split_axis=0,
        concat_axis=0,
        tiled=True,
    )
    tag_rows = lax.all_to_all(tag_out, "expert", split_axis=0, concat_axis=0, tiled=True)
    routed = lax.all_gather(arrived.reshape(-1, arrived.shape[2]), "blk", axis=1, tiled=True)
    tag_rows = tag_rows.reshape(-1)
    gate_pre = jnp.dot(routed, gate_weight[0], preferred_element_type=jnp.float32)
    up_pre = jnp.dot(routed, up_weight[0], preferred_element_type=jnp.float32)
    hidden = (jax.nn.silu(gate_pre) * up_pre).astype(jnp.bfloat16)
    live_count = jnp.sum((tag_rows > 0).astype(jnp.float32))
    class_ids = jnp.arange(CLASSES, dtype=jnp.int32)
    one_hot = (tag_rows[:, None] - 1 == class_ids[None, :]).astype(jnp.bfloat16)
    contract_rows = (((0,), (0,)), ((), ()))
    cross_cov = lax.dot_general(
        hidden, one_hot, contract_rows, preferred_element_type=jnp.float32
    ) * (CLASSES / live_count)
    moment = (
        lax.dot_general(
            hidden,
            lax.all_gather(hidden, "blk", axis=1, tiled=True),
            contract_rows,
            preferred_element_type=jnp.float32,
        )
        / live_count
    ).astype(jnp.bfloat16)
    return (moment[None], cross_cov[None])


def solution(mesh):
    in_specs = (
        P("expert", "blk"),
        P("expert", None),
        P("expert"),
        P("expert", None, "blk"),
        P("expert", None, "blk"),
    )
    out_specs = (P("expert", "blk", None), P("expert", "blk", None))
    return jax.shard_map(shards, mesh=mesh, in_specs=in_specs, out_specs=out_specs, check_vma=False)
```

profile of v0, /device:TPU:0, one launch (start us, length us, event | category | flops | bytes accessed | tf_op | source)
XLA Modules:
  0.0 177.5 jit_solution(7608917219000824664)
XLA Ops:
  7.2 0.0 copy-start
  7.2 0.0 all-gather.3.cloned.1.call-start
  7.2 0.7 fusion.14
  7.9 0.1 copy.19
  8.0 0.2 reduce_window_sum.11
  8.2 0.1 copy.20
  8.3 0.0 copy-done
  8.3 0.3 convolution_convert_fusion
  8.6 12.2 %all_to_all.14 = bf16[4,128,384]{2,1,0:T(8,128)(2,1)} all-to-all(bf16[4,128,384]{2,1,0:T(8,128)(2,1)S(1)} %convolution_convert_fusion), channel_id=1, replica_groups=mesh['expert'=4,'blk'=8] {'expert'}, dimensions={0} | all-to-all | bytes 786432 | tf_op jit(solution)/shard_map/all_to_all | solution.py:21
  20.8 0.0 all-gather.3.cloned.1.call-update
  20.8 0.0 all-gather.5.cloned.1.call-start
  20.8 38.1 %all-gather.3.cloned.1.call-done = bf16[512,3072]{1,0:T(8,128)(2,1)} async-done(((bf16[512,384]{1,0:T(8,128)(2,1)}), bf16[512,3072]{1,0:T(8,128)(2,1)}) %all-gather.3.cloned.1.call-update) | async-done | bytes 3145744 | tf_op jit(solution)/shard_map/all_gather | solution.py:31
  58.9 0.0 copy-start.1
  58.9 7.3 %fusion.1 = f32[512,1024]{1,0:T(8,128)S(1)} fusion(bf16[512,3072]{1,0:T(8,128)(2,1)} %all-gather.3.cloned.1.call-done, bf16[1,3072,1024]{2,1,0:T(8,128)(2,1)} %param.9), kind=kOutput, calls=%fused_computation.2 | convolution fusion | flops 3221225472 | bytes 11534336 | tf_op jit(solution)/shard_map/dot_general | solution.py:34
  66.2 0.0 copy-done.1
  66.2 0.0 copy-start.2
  66.2 7.6 %multiply_convert_fusion = bf16[512,1024]{1,0:T(8,128)(2,1)} fusion(f32[512,1024]{1,0:T(8,128)S(1)} %fusion.1, bf16[512,3072]{1,0:T(8,128)(2,1)S(1)} %copy-done.1, bf16[1,3072,1024]{2,1,0:T(8,128)(2,1)} %param.8), kind=kOutput, calls=%fused_computation.6 | convolution fusion | flops 3224371200 | bytes 12582912 | tf_op jit(solution)/shard_map/dot_general | solution.py:33
  73.8 0.0 all-gather.5.cloned.1.call-update
  73.8 0.0 copy-done.2
  73.9 0.1 select_reduce_fusion
  74.0 8.1 %all_to_all.15 = s32[4,1,128]{2,1,0:T(1,128)S(1)} all-to-all(s32[4,1,128]{2,1,0:T(1,128)S(1)} %bitcast.29), channel_id=1, replica_groups=mesh['expert'=4,'blk'=8] {'expert'}, dimensions={0} | all-to-all | bytes 4096 | tf_op jit(solution)/shard_map/all_to_all | solution.py:30
  82.1 0.7 fusion.15
  83.4 2.3 %fusion.7 = f32[1,1024,16]{1,2,0:T(8,128)} fusion(bf16[512,1024]{1,0:T(8,128)(2,1)} %multiply_convert_fusion, s32[512]{0:T(512)S(1)} %bitcast.28, f32[]{:T(128)S(6)} %div.16), kind=kOutput, calls=%fused_computation.9 | convolution fusion | flops 16801792 | bytes 1116164 | tf_op jit(solution)/shard_map/dot_general | solution.py:40
  85.7 69.3 %all-gather.5.cloned.1.call-done = bf16[512,8192]{1,0:T(8,128)(2,1)} async-done(((bf16[512,1024]{1,0:T(8,128)(2,1)}), bf16[512,8192]{1,0:T(8,128)(2,1)}) %all-gather.5.cloned.1.call-update) | async-done | bytes 8388624 | tf_op jit(solution)/shard_map/all_gather | solution.py:46
  155.0 15.7 %fusion = bf16[1,1024,8192]{2,1,0:T(8,128)(2,1)} fusion(f32[]{:T(128)} %fusion.15, bf16[512,1024]{1,0:T(8,128)(2,1)} %multiply_convert_fusion, bf16[512,8192]{1,0:T(8,128)(2,1)} %all-gather.5.cloned.1.call-done), kind=kOutput, calls=%fused_computation.1 | convolution fusion | flops 8606711808 | bytes 26214404 | tf_op jit(solution)/shard_map/dot_general | solution.py:44
  (4 shorter events, 0.0 us)
Async XLA Ops:
  7.2 1.1 copy-start
  7.2 51.7 %all-gather.3.cloned.1.call-start = ((), (), s32[]{:S(2)}) async-start(), calls=%async_computation.2 | async-start | bytes 3538944 | tf_op jit(solution)/shard_map/all_gather | solution.py:31
  20.8 134.2 %all-gather.5.cloned.1.call-start = ((), (), s32[]{:S(2)}) async-start(), calls=%async_computation.3 | async-start | bytes 9437184 | tf_op jit(solution)/shard_map/all_gather | solution.py:46
  58.9 7.3 %copy-start.1 = (bf16[512,3072]{1,0:T(8,128)(2,1)S(1)}, bf16[512,3072]{1,0:T(8,128)(2,1)}, u32[]{:S(2)}) copy-start(bf16[512,3072]{1,0:T(8,128)(2,1)} %all-gather.3.cloned.1.call-done) | copy-start | bytes 9437188
  66.2 7.7 %copy-start.2 = (s32[128]{0:T(128)S(1)}, s32[128]{0:T(128)}, u32[]{:S(2)}) copy-start(s32[128]{0:T(128)} %param.7) | copy-start | bytes 1540
Sparse Core Ops, SparseCore 0:
  20.9 37.9 all-gather.2
  74.0 80.9 all-gather.4
where the time goes:
time: 178 us
  waiting for transfers between devices  107 us (60%)
  matrix products  33.1 us (19%)
  blocking collectives  20.3 us (11%)
  between operations  14.8 us (8%)
    all_gather x1, waiting for transfers between devices, shards(): lax.all_gather(hidden, 'blk', axis=1, tiled=True)  69.3 us
    all_gather x1, waiting for transfers between devices, shards(): lax.all_gather(arrived.reshape(-1, arrived.shape[2]), 'blk', axis=1, tile...  38.1 us
    dot_general x1, matrix products, shards(): lax.dot_general(hidden, lax.all_gather(hidden, 'blk', axis=1, tiled=True)...  15.7 us
    all_to_all x1, blocking collectives, shards(): lax.all_to_all(jnp.einsum('est,td->esd', select_mat, tokens, preferred_el...  12.2 us
    all_to_all x1, blocking collectives, shards(): lax.all_to_all(tag_out, 'expert', split_axis=0, concat_axis=0, tiled=True)  8.09 us
    dot_general x1, matrix products, shards(): jnp.dot(routed, gate_weight[0], preferred_element_type=jnp.float32)  7.61 us
    dot_general x1, matrix products, shards(): up_pre = jnp.dot(routed, up_weight[0], preferred_element_type=jnp.float32)  7.26 us
  transfers between devices with their start and end apart: 2, of which 2 were waited for; matrix products, arithmetic and copies ran while one was open for 2% of the time, Pallas kernels for 0%

commit v1 on v0

v1 whole, which is shorter than its diff:
```python
import functools

import jax
import jax.numpy as jnp
from jax import lax
from jax.experimental import pallas as pl
from jax.experimental.pallas import tpu as pltpu
from jax.sharding import PartitionSpec as P

CLASSES = 16
MIB = 1 << 20
MESH = pl.DeviceIdType.MESH


def gather_kernel(E, B, t_ref, meta_ref, wg_ref, wu_ref, h_ref, m_ref,
                  tok, wg, wu, own, loc_sem, own_sem, tz_s, tsib_s, tpl_s, t_r, m_s, m_r,
                  hsib_s, hup_s, hdn_s, h_r):
    Z = B // 2
    rows, F = t_ref.shape
    W = wg_ref.shape[2]
    e, b = lax.axis_index("expert"), lax.axis_index("blk")
    z, c = b // 2, b % 2
    sib = b + 1 - 2 * c

    g_copy = pltpu.make_async_copy(wg_ref.at[0], wg, loc_sem.at[0])
    u_copy = pltpu.make_async_copy(wu_ref.at[0], wu, loc_sem.at[1])
    g_copy.start()
    u_copy.start()

    barrier = pltpu.get_barrier_semaphore()

    def to(expert, blk):
        return {"expert": expert, "blk": blk}

    def greet(expert, blk):
        pl.semaphore_signal(barrier, inc=1, device_id=to(expert, blk), device_id_type=MESH)

    greet(e, sib)
    for d in range(1, Z):
        greet(e, 2 * lax.rem(z + d, Z) + c)
    for k in range(1, E):
        greet(lax.rem(e + k, E), b)
    pl.semaphore_wait(barrier, Z + E - 1)

    def chunk(s, blk):
        return tok.at[s, :, pl.ds(pl.multiple_of(blk * F, 128), F)]

    def piece(s, blk):
        return h_ref.at[pl.ds(pl.multiple_of(s * rows, rows), rows), pl.ds(pl.multiple_of(blk * W, 128), W)]

    def remote(src, dst, send, recv, expert, blk):
        return pltpu.make_async_remote_copy(
            src_ref=src, dst_ref=dst, send_sem=send, recv_sem=recv,
            device_id=to(expert, blk), device_id_type=MESH)

    def tok_z(d):
        return remote(t_ref, chunk(e, b), tz_s.at[d], t_r.at[e, b], e, 2 * lax.rem(z + d, Z) + c)

    def tok_sib(s, zz, src=None):
        blk = 2 * zz + c
        return remote(chunk(s, blk) if src is None else src, chunk(s, blk), tsib_s.at[s, zz], t_r.at[s, blk], e, sib)

    def tok_plane(k, zz, src=None):
        blk = 2 * zz + c
        return remote(chunk(e, blk) if src is None else src, chunk(e, blk), tpl_s.at[k, zz], t_r.at[e, blk],
                      lax.rem(e + k, E), b)

    def tok_here(s, blk):
        remote(chunk(s, blk), chunk(s, blk), tz_s.at[0], t_r.at[s, blk], e, sib).wait_recv()

    def meta_to(k):
        return remote(meta_ref, m_ref.at[e], m_s.at[k], m_r.at[e], lax.rem(e + k, E), b)

    t_copy = pltpu.make_async_copy(t_ref, chunk(e, b), loc_sem.at[2])
    m_copy = pltpu.make_async_copy(meta_ref, m_ref.at[e], loc_sem.at[3])
    for d in range(1, Z):
        tok_z(d).start()
    tok_sib(e, z, t_ref).start()
    for k in range(1, E):
        tok_plane(k, z, t_ref).start()
    t_copy.start()
    m_copy.start()
    for k in range(1, E):
        meta_to(k).start()

    def h_sib(s, zz, src=None):
        blk = 2 * zz + c
        return remote(piece(s, blk) if src is None else src, piece(s, blk), hsib_s.at[s, zz], h_r.at[s, blk], e, sib)

    def h_up(s, zz, src=None):
        blk = 2 * zz + c
        return remote(piece(s, blk) if src is None else src, piece(s, blk), hup_s.at[s, zz], h_r.at[s, blk], e, b + 2)

    def h_dn(s, zz, src=None):
        blk = 2 * zz + c
        return remote(piece(s, blk) if src is None else src, piece(s, blk), hdn_s.at[s, zz], h_r.at[s, blk], e, b - 2)

    def h_here(s, blk):
        remote(piece(s, blk), piece(s, blk), hsib_s.at[s, 0], h_r.at[s, blk], e, sib).wait_recv()

    def own_copy(s):
        return pltpu.make_async_copy(own.at[s], piece(s, b), own_sem.at[s])

    tile = min(W, 256)

    def compute(j, s):
        @pl.when(j == 0)
        def _():
            def arrived(d, carry):
                zz = lax.rem(z + d, Z)
                tok_here(e, 2 * zz + c)
                tok_sib(e, zz).start()
                for k in range(1, E):
                    tok_plane(k, zz).start()
                return carry

            lax.fori_loop(1, Z, arrived, 0)
            t_copy.wait()
            g_copy.wait()
            u_copy.wait()

        @pl.when(j > 0)
        def _():
            def arrived(d, carry):
                zz = lax.rem(z + d, Z)
                tok_here(s, 2 * zz + c)
                tok_sib(s, zz).start()
                return carry

            lax.fori_loop(0, Z, arrived, 0)

        def other(zz, carry):
            tok_here(s, 2 * zz + 1 - c)
            return carry

        lax.fori_loop(0, Z, other, 0)

        def columns(i, carry):
            cols = pl.ds(pl.multiple_of(i * tile, tile), tile)
            x = tok[s]
            gate = jnp.dot(x, wg[:, cols], preferred_element_type=jnp.float32)
            up = jnp.dot(x, wu[:, cols], preferred_element_type=jnp.float32)
            own[s, :, cols] = (gate / (1.0 + jnp.exp(-gate)) * up).astype(own.dtype)
            return carry

        lax.fori_loop(0, W // tile, columns, 0)

        @pl.when(z < Z - 1)
        def _():
            h_up(s, z, own.at[s]).start()

        @pl.when(z > 0)
        def _():
            h_dn(s, z, own.at[s]).start()

        h_sib(s, z, own.at[s]).start()
        own_copy(s).start()

    def forward(s, d):
        @pl.when(z - d >= 0)
        def _():
            h_here(s, 2 * (z - d) + c)

            @pl.when(z < Z - 1)
            def _():
                h_up(s, z - d).start()

            h_sib(s, z - d).start()

        @pl.when(z + d < Z)
        def _():
            h_here(s, 2 * (z + d) + c)

            @pl.when(z > 0)
            def _():
                h_dn(s, z + d).start()

            h_sib(s, z + d).start()

    def turn(k, carry):
        def inner(i, carry):
            j = E - 1 - i
            s = lax.rem(e + j, E)
            d = k - j

            @pl.when(d == 0)
            def _():
                compute(j, s)

            @pl.when((d > 0) & (d < Z))
            def _():
                forward(s, d)

            return carry

        return lax.fori_loop(0, E, inner, carry)

    lax.fori_loop(0, E + Z - 1, turn, 0)

    m_copy.wait()
    for d in range(1, Z):
        tok_z(d).wait_send()
    for k in range(1, E):
        meta_to(k).wait_send()
        other = lax.rem(e + k, E)
        remote(meta_ref, m_ref.at[other], m_s.at[k], m_r.at[other], other, b).wait_recv()

    def finish(s, carry):
        own_copy(s).wait()

        def chips(zz, carry):
            h_here(s, 2 * zz + 1 - c)
            tok_sib(s, zz).wait_send()
            h_sib(s, zz).wait_send()

            @pl.when(s > 0)
            def _():
                tok_plane(s, zz).wait_send()

            @pl.when((zz <= z) & (z < Z - 1))
            def _():
                h_up(s, zz).wait_send()

            @pl.when((zz >= z) & (z > 0))
            def _():
                h_dn(s, zz).wait_send()

            return carry

        return lax.fori_loop(0, Z, chips, carry)

    lax.fori_loop(0, E, finish, 0)


def gather(tokens, meta, gate_weight, up_weight, E, B):
    rows, F = tokens.shape
    D, W = gate_weight.shape[1:]
    Z = B // 2
    anywhere = pl.BlockSpec(memory_space=pl.ANY)
    dma = pltpu.SemaphoreType.DMA
    return pl.pallas_call(
        functools.partial(gather_kernel, E, B),
        out_shape=[jax.ShapeDtypeStruct((E * rows, B * W), jnp.bfloat16),
                   jax.ShapeDtypeStruct((E,) + meta.shape, jnp.int32)],
        in_specs=[anywhere] * 4,
        out_specs=[anywhere] * 2,
        scratch_shapes=[
            pltpu.VMEM((E, rows, D), jnp.bfloat16),
            pltpu.VMEM((D, W), jnp.bfloat16),
            pltpu.VMEM((D, W), jnp.bfloat16),
            pltpu.VMEM((E, rows, W), jnp.bfloat16),
            dma((4,)), dma((E,)), dma((Z,)), dma((E, Z)), dma((E, Z)), dma((E, B)), dma((E,)), dma((E,)),
            dma((E, Z)), dma((E, Z)), dma((E, Z)), dma((E, B)),
        ],
        compiler_params=pltpu.CompilerParams(
            collective_id=0, has_side_effects=True, vmem_limit_bytes=40 * MIB),
        name="gather_hidden",
    )(tokens, meta, gate_weight, up_weight)


def moment_kernel(E, place, meta_ref, own_ref, all_ref, moment_ref, cross_ref, lhs, scale):
    @pl.when(pl.program_id(0) == 0)
    def _():
        e = place[0]

        def row(i):
            return jnp.concatenate([meta_ref[s, i:i + 1, :] for s in range(E)], axis=1)

        live = (row(0) == e) | (row(1) == e)
        count = jnp.sum(live.astype(jnp.float32), axis=1, keepdims=True)
        flipped = own_ref[...].T
        masked = flipped * live.astype(jnp.bfloat16)
        lhs[...] = masked
        classes = lax.broadcasted_iota(jnp.int32, (CLASSES, live.shape[1]), 0)
        one_hot = ((row(2) == classes) & live).astype(jnp.bfloat16)
        scale[...] = jnp.broadcast_to(1.0 / count, scale.shape)
        cross_ref[...] = lax.dot_general(
            one_hot, masked, (((1,), (1,)), ((), ())), preferred_element_type=jnp.float32) * (CLASSES / count)

    acc = jnp.dot(lhs[...], all_ref[...], preferred_element_type=jnp.float32)
    moment_ref[0] = (acc * scale[0:1, 0:1]).astype(moment_ref.dtype)


def moments(place, meta, hidden, E, B):
    rows, FF = hidden.shape
    W = FF // B
    tile = 512
    return pl.pallas_call(
        functools.partial(moment_kernel, E),
        grid_spec=pltpu.PrefetchScalarGridSpec(
            num_scalar_prefetch=1,
            grid=(FF // tile,),
            in_specs=[
                pl.BlockSpec(meta.shape, lambda i, p: (0, 0, 0)),
                pl.BlockSpec((rows, W), lambda i, p: (0, p[1])),
                pl.BlockSpec((rows, tile), lambda i, p: (0, i)),
            ],
            out_specs=[
                pl.BlockSpec((1, W, tile), lambda i, p: (0, 0, i)),
                pl.BlockSpec((CLASSES, W), lambda i, p: (0, 0)),
            ],
            scratch_shapes=[pltpu.VMEM((W, rows), jnp.bfloat16), pltpu.VMEM((8, 128), jnp.float32)],
        ),
        out_shape=[jax.ShapeDtypeStruct((1, W, FF), jnp.bfloat16), jax.ShapeDtypeStruct((CLASSES, W), jnp.float32)],
        compiler_params=pltpu.CompilerParams(vmem_limit_bytes=40 * MIB),
        name="moments",
    )(place, meta, hidden, hidden)


def plain(tokens, routes, labels, gate_weight, up_weight):
    everyone = lax.all_gather(lax.all_gather(tokens, "expert", axis=0, tiled=True), "blk", axis=1, tiled=True)
    routes = lax.all_gather(routes, "expert", axis=0, tiled=True)
    labels = lax.all_gather(labels, "expert", axis=0, tiled=True)
    live = jnp.any(routes == lax.axis_index("expert"), axis=1)
    gate = jnp.dot(everyone, gate_weight[0], preferred_element_type=jnp.float32)
    up = jnp.dot(everyone, up_weight[0], preferred_element_type=jnp.float32)
    hidden = jnp.where(live[:, None], jax.nn.silu(gate) * up, 0).astype(jnp.bfloat16)
    count = jnp.sum(live.astype(jnp.float32))
    one_hot = (labels[:, None] == jnp.arange(CLASSES, dtype=jnp.int32)[None, :]).astype(jnp.bfloat16)
    over_rows = (((0,), (0,)), ((), ()))
    cross = lax.dot_general(hidden, one_hot, over_rows, preferred_element_type=jnp.float32) * (CLASSES / count)
    full = lax.all_gather(hidden, "blk", axis=1, tiled=True)
    moment = lax.dot_general(hidden, full, over_rows, preferred_element_type=jnp.float32) / count
    return moment.astype(jnp.bfloat16)[None], cross[None]


def shards(tokens, routes, labels, gate_weight, up_weight):
    E, B = lax.axis_size("expert"), lax.axis_size("blk")
    rows, F = tokens.shape
    W = gate_weight.shape[2]
    if B % 2 or F % 128 or W % 256 or rows != 128:
        return plain(tokens, routes, labels, gate_weight, up_weight)
    meta = jnp.concatenate([routes.T, labels[None], jnp.zeros((5, rows), jnp.int32)], axis=0)
    hidden, meta_all = gather(tokens, meta, gate_weight, up_weight, E, B)
    place = jnp.stack([lax.axis_index("expert"), lax.axis_index("blk")]).astype(jnp.int32)
    moment, cross = moments(place, meta_all, hidden, E, B)
    return moment, cross.T[None]


def solution(mesh):
    in_specs = (
        P("expert", "blk"),
        P("expert", None),
        P("expert"),
        P("expert", None, "blk"),
        P("expert", None, "blk"),
    )
    out_specs = (P("expert", "blk", None), P("expert", "blk", None))
    return jax.shard_map(shards, mesh=mesh, in_specs=in_specs, out_specs=out_specs, check_vma=False)
```

time: 178 us -> 126 us (0.71)
  Pallas kernels: 0 us -> 114 us
  waiting for transfers between devices: 107 us -> 0 us
  matrix products: 33.1 us -> 0 us
  blocking collectives: 20.3 us -> 0 us
  between operations: 14.8 us -> 0.66 us
  local copies, waits for them, and re-layouts: 0.19 us -> 9.91 us
    pallas_call x0 -> x2, Pallas kernels: none -> 114 us  [the longest x1 98.5 us: gather(): pl.pallas_call(functools.partial(gather_kernel, E, B), out_shape=[jax.Sha...]
    all_gather x2 -> x0, waiting for transfers between devices: 107 us -> none  [the longest x1 69.3 us: shards(): lax.all_gather(hidden, 'blk', axis=1, tiled=True)]
    dot_general x5 -> x0, matrix products: 33.1 us -> none  [the longest x1 15.7 us: shards(): lax.dot_general(hidden, lax.all_gather(hidden, 'blk', axis=1, tiled=True)...]
    all_to_all x2 -> x0, blocking collectives: 20.3 us -> none  [the longest x1 12.2 us: shards(): lax.all_to_all(jnp.einsum('est,td->esd', select_mat, tokens, preferred_el...]
    unnamed x6 -> x8, local copies, waits for them, and re-layouts: 0.02 us -> 9.84 us
  transfers between devices with their start and end apart: 2 -> 0, of which waited for: 2 -> 0; matrix products, arithmetic and copies ran while one was open for 2% -> 0% of each run, Pallas kernels for 0% -> 0%
where the time goes in v1:
time: 126 us
  Pallas kernels  114 us (90%)
  local copies, waits for them, and re-layouts  9.91 us (8%)
    pallas_call x1, Pallas kernels, gather(): pl.pallas_call(functools.partial(gather_kernel, E, B), out_shape=[jax.Sha...  98.5 us
    pallas_call x1, Pallas kernels, moments(): pl.pallas_call(functools.partial(moment_kernel, E), grid_spec=pltpu.Prefe...  15.7 us
    unnamed x8, local copies, waits for them, and re-layouts  9.84 us

profile of v1, /device:TPU:0, one launch (start us, length us, event | category | flops | bytes accessed | tf_op | source)
XLA Modules:
  0.0 125.6 jit_solution(6518941139730992374)
XLA Ops:
  0.6 0.1 pad_add_fusion.place
  0.7 0.1 pad.2.clone
  0.8 0.8 add_add_fusion.meta_ref
  1.6 0.0 copy-start.1
  1.6 2.8 %copy-done.1 = bf16[1,3072,1024]{2,1,0:T(8,128)(2,1)S(1)} copy-done((bf16[1,3072,1024]{2,1,0:T(8,128)(2,1)S(1)}, bf16[1,3072,1024]{2,1,0:T(8,128)(2,1)}, u32[]{:S(2)}) %copy-start.1) | copy-done | bytes 6291480
  4.3 0.0 copy-start.2
  4.3 2.8 %copy-done.2 = bf16[1,3072,1024]{2,1,0:T(8,128)(2,1)S(1)} copy-done((bf16[1,3072,1024]{2,1,0:T(8,128)(2,1)S(1)}, bf16[1,3072,1024]{2,1,0:T(8,128)(2,1)}, u32[]{:S(2)}) %copy-start.2) | copy-done | bytes 6291480
  7.1 0.0 copy-start.3
  7.1 0.9 copy-done.3
  8.0 98.5 %gather_hidden.1 = (bf16[512,8192]{1,0:T(8,128)(2,1)}, s32[4,8,128]{2,1,0:T(8,128)S(1)}) custom-call(bf16[128,384]{1,0:T(8,128)(2,1)S(1)} %copy-done.3, s32[8,128]{1,0:T(8,128)S(1)} %add_add_fusion.meta_ref, bf16[1,3072,1024]{2,1,0:T(8,128)(2,1)S(1)} %copy-done.1, bf16[1,3072,1024]{2,1,0:T(8,128)(2,1)S(1)} %copy-done.2), custom_call_target="tpu_custom_call" | custom-call | tf_op jit(solution)/shard_map/gather_hidden/pallas_call | solution.py:241
  106.5 0.0 copy-start
  106.5 3.4 %copy-done = bf16[512,8192]{1,0:T(8,128)(2,1)S(1)} copy-done((bf16[512,8192]{1,0:T(8,128)(2,1)S(1)}, bf16[512,8192]{1,0:T(8,128)(2,1)}, u32[]{:S(2)}) %copy-start) | copy-done | bytes 8388632
  109.9 15.7 %moments.1 = (bf16[1,1024,8192]{2,1,0:T(8,128)(2,1)}, f32[16,1024]{1,0:T(8,128)}) custom-call(s32[2]{0:T(128)S(1)} %pad_add_fusion.place, s32[4,8,128]{2,1,0:T(8,128)S(1)} %get-tuple-element.6.meta_ref, bf16[512,8192]{1,0:T(8,128)(2,1)S(1)} %copy-done, bf16[512,8192]{1,0:T(8,128)(2,1)S(1)} %copy-done), custom_call_target="tpu_custom_call" | custom-call | tf_op jit(solution)/shard_map/moments/pallas_call | solution.py:288
  (1 shorter events, 0.0 us)
Async XLA Ops:
  1.6 2.8 %copy-start.1 = (bf16[1,3072,1024]{2,1,0:T(8,128)(2,1)S(1)}, bf16[1,3072,1024]{2,1,0:T(8,128)(2,1)}, u32[]{:S(2)}) copy-start(bf16[1,3072,1024]{2,1,0:T(8,128)(2,1)} %wg_ref.1) | copy-start | bytes 18874372
  4.3 2.8 %copy-start.2 = (bf16[1,3072,1024]{2,1,0:T(8,128)(2,1)S(1)}, bf16[1,3072,1024]{2,1,0:T(8,128)(2,1)}, u32[]{:S(2)}) copy-start(bf16[1,3072,1024]{2,1,0:T(8,128)(2,1)} %wu_ref.1) | copy-start | bytes 18874372
  7.1 0.9 copy-start.3
  106.5 3.4 %copy-start = (bf16[512,8192]{1,0:T(8,128)(2,1)S(1)}, bf16[512,8192]{1,0:T(8,128)(2,1)}, u32[]{:S(2)}) copy-start(bf16[512,8192]{1,0:T(8,128)(2,1)} %get-tuple-element.7.own_ref.all_ref) | copy-start | bytes 25165828

commit v2 on v1

--- a/solution.py
+++ b/solution.py
@@ -12,8 +12,8 @@
 MESH = pl.DeviceIdType.MESH
 
 
-def gather_kernel(E, B, t_ref, meta_ref, wg_ref, wu_ref, h_ref, m_ref,
-                  tok, wg, wu, own, loc_sem, own_sem, tz_s, tsib_s, tpl_s, t_r, m_s, m_r,
+def gather_kernel(E, B, t_ref, meta_ref, wg_ref, wu_ref, moment_ref, cross_ref,
+                  tok, wg, wu, h_ref, m_ref, lhs, scale, loc_sem, tz_s, tsib_s, tpl_s, t_r, m_s, m_r,
                   hsib_s, hup_s, hdn_s, h_r):
     Z = B // 2
     rows, F = t_ref.shape
@@ -83,23 +83,20 @@
     for k in range(1, E):
         meta_to(k).start()
 
-    def h_sib(s, zz, src=None):
-        blk = 2 * zz + c
-        return remote(piece(s, blk) if src is None else src, piece(s, blk), hsib_s.at[s, zz], h_r.at[s, blk], e, sib)
-
-    def h_up(s, zz, src=None):
-        blk = 2 * zz + c
-        return remote(piece(s, blk) if src is None else src, piece(s, blk), hup_s.at[s, zz], h_r.at[s, blk], e, b + 2)
-
-    def h_dn(s, zz, src=None):
-        blk = 2 * zz + c
-        return remote(piece(s, blk) if src is None else src, piece(s, blk), hdn_s.at[s, zz], h_r.at[s, blk], e, b - 2)
+    def h_sib(s, zz):
+        blk = 2 * zz + c
+        return remote(piece(s, blk), piece(s, blk), hsib_s.at[s, zz], h_r.at[s, blk], e, sib)
+
+    def h_up(s, zz):
+        blk = 2 * zz + c
+        return remote(piece(s, blk), piece(s, blk), hup_s.at[s, zz], h_r.at[s, blk], e, b + 2)
+
+    def h_dn(s, zz):
+        blk = 2 * zz + c
+        return remote(piece(s, blk), piece(s, blk), hdn_s.at[s, zz], h_r.at[s, blk], e, b - 2)
 
     def h_here(s, blk):
         remote(piece(s, blk), piece(s, blk), hsib_s.at[s, 0], h_r.at[s, blk], e, sib).wait_recv()
-
-    def own_copy(s):
-        return pltpu.make_async_copy(own.at[s], piece(s, b), own_sem.at[s])
 
     tile = min(W, 256)
 
@@ -140,21 +137,22 @@
             x = tok[s]
             gate = jnp.dot(x, wg[:, cols], preferred_element_type=jnp.float32)
             up = jnp.dot(x, wu[:, cols], preferred_element_type=jnp.float32)
-            own[s, :, cols] = (gate / (1.0 + jnp.exp(-gate)) * up).astype(own.dtype)
+            h_ref[pl.ds(pl.multiple_of(s * rows, rows), rows),
+                  pl.ds(pl.multiple_of(b * W + i * tile, 128), tile)] = (
+                gate / (1.0 + jnp.exp(-gate)) * up).astype(h_ref.dtype)
             return carry
 
         lax.fori_loop(0, W // tile, columns, 0)
 
         @pl.when(z < Z - 1)
         def _():
-            h_up(s, z, own.at[s]).start()
+            h_up(s, z).start()
 
         @pl.when(z > 0)
         def _():
-            h_dn(s, z, own.at[s]).start()
-
-        h_sib(s, z, own.at[s]).start()
-        own_copy(s).start()
+            h_dn(s, z).start()
+
+        h_sib(s, z).start()
 
     def forward(s, d):
         @pl.when(z - d >= 0)
@@ -193,83 +191,41 @@
 
             return carry
 
-        return lax.fori_loop(0, E, inner, carry)
-
-    lax.fori_loop(0, E + Z - 1, turn, 0)
-
-    m_copy.wait()
-    for d in range(1, Z):
-        tok_z(d).wait_send()
-    for k in range(1, E):
-        meta_to(k).wait_send()
-        other = lax.rem(e + k, E)
-        remote(meta_ref, m_ref.at[other], m_s.at[k], m_r.at[other], other, b).wait_recv()
-
-    def finish(s, carry):
-        own_copy(s).wait()
-
-        def chips(zz, carry):
-            h_here(s, 2 * zz + 1 - c)
-            tok_sib(s, zz).wait_send()
-            h_sib(s, zz).wait_send()
-
-            @pl.when(s > 0)
-            def _():
-                tok_plane(s, zz).wait_send()
-
-            @pl.when((zz <= z) & (z < Z - 1))
-            def _():
-                h_up(s, zz).wait_send()
-
-            @pl.when((zz >= z) & (z > 0))
-            def _():
-                h_dn(s, zz).wait_send()
-
-            return carry
-
-        return lax.fori_loop(0, Z, chips, carry)
-
-    lax.fori_loop(0, E, finish, 0)
-
-
-def gather(tokens, meta, gate_weight, up_weight, E, B):
-    rows, F = tokens.shape
-    D, W = gate_weight.shape[1:]
-    Z = B // 2
-    anywhere = pl.BlockSpec(memory_space=pl.ANY)
-    dma = pltpu.SemaphoreType.DMA
-    return pl.pallas_call(
-        functools.partial(gather_kernel, E, B),
-        out_shape=[jax.ShapeDtypeStruct((E * rows, B * W), jnp.bfloat16),
-                   jax.ShapeDtypeStruct((E,) + meta.shape, jnp.int32)],
-        in_specs=[anywhere] * 4,
-        out_specs=[anywhere] * 2,
-        scratch_shapes=[
-            pltpu.VMEM((E, rows, D), jnp.bfloat16),
-            pltpu.VMEM((D, W), jnp.bfloat16),
-            pltpu.VMEM((D, W), jnp.bfloat16),
-            pltpu.VMEM((E, rows, W), jnp.bfloat16),
-            dma((4,)), dma((E,)), dma((Z,)), dma((E, Z)), dma((E, Z)), dma((E, B)), dma((E,)), dma((E,)),
-            dma((E, Z)), dma((E, Z)), dma((E, Z)), dma((E, B)),
-        ],
-        compiler_params=pltpu.CompilerParams(
-            collective_id=0, has_side_effects=True, vmem_limit_bytes=40 * MIB),
-        name="gather_hidden",
-    )(tokens, meta, gate_weight, up_weight)
-
-
-def moment_kernel(E, place, meta_ref, own_ref, all_ref, moment_ref, cross_ref, lhs, scale):
-    @pl.when(pl.program_id(0) == 0)
-    def _():
-        e = place[0]
+        lax.fori_loop(0, E, inner, 0)
+        d = k - (E - 1)
+
+        @pl.when(d == 0)
+        def _():
+            prepare()
+            block(b)
+
+        @pl.when(d > 0)
+        def _():
+            @pl.when(z - d >= 0)
+            def _():
+                block(2 * (z - d) + c)
+
+            @pl.when(z + d < Z)
+            def _():
+                block(2 * (z + d) + c)
+
+            from_sibling(d - 1)
+
+        return carry
+
+    def prepare():
+        m_copy.wait()
+        for k in range(1, E):
+            meta_to(k).wait_send()
+            other = lax.rem(e + k, E)
+            remote(meta_ref, m_ref.at[other], m_s.at[k], m_r.at[other], other, b).wait_recv()
 
         def row(i):
-            return jnp.concatenate([meta_ref[s, i:i + 1, :] for s in range(E)], axis=1)
+            return jnp.concatenate([m_ref[s, i:i + 1, :] for s in range(E)], axis=1)
 
         live = (row(0) == e) | (row(1) == e)
         count = jnp.sum(live.astype(jnp.float32), axis=1, keepdims=True)
-        flipped = own_ref[...].T
-        masked = flipped * live.astype(jnp.bfloat16)
+        masked = h_ref[:, pl.ds(pl.multiple_of(b * W, 128), W)].T * live.astype(jnp.bfloat16)
         lhs[...] = masked
         classes = lax.broadcasted_iota(jnp.int32, (CLASSES, live.shape[1]), 0)
         one_hot = ((row(2) == classes) & live).astype(jnp.bfloat16)
@@ -277,34 +233,91 @@
         cross_ref[...] = lax.dot_general(
             one_hot, masked, (((1,), (1,)), ((), ())), preferred_element_type=jnp.float32) * (CLASSES / count)
 
-    acc = jnp.dot(lhs[...], all_ref[...], preferred_element_type=jnp.float32)
-    moment_ref[0] = (acc * scale[0:1, 0:1]).astype(moment_ref.dtype)
-
-
-def moments(place, meta, hidden, E, B):
-    rows, FF = hidden.shape
-    W = FF // B
-    tile = 512
+    def block(blk):
+        def columns(i, carry):
+            cols = pl.ds(pl.multiple_of(blk * W + i * tile, 128), tile)
+            acc = jnp.dot(lhs[...], h_ref[:, cols], preferred_element_type=jnp.float32)
+            moment_ref[0, :, cols] = (acc * scale[0:1, 0:1]).astype(moment_ref.dtype)
+            return carry
+
+        lax.fori_loop(0, W // tile, columns, 0)
+
+    def from_sibling(d):
+        def arrived(zz):
+            blk = 2 * zz + 1 - c
+
+            def shard(s, carry):
+                h_here(s, blk)
+                return carry
+
+            lax.fori_loop(0, E, shard, 0)
+            block(blk)
+
+        @pl.when(z - d >= 0)
+        def _():
+            arrived(z - d)
+
+        @pl.when((d > 0) & (z + d < Z))
+        def _():
+            arrived(z + d)
+
+    lax.fori_loop(0, E + Z - 1, turn, 0)
+    from_sibling(Z - 1)
+
+    for d in range(1, Z):
+        tok_z(d).wait_send()
+
+    def finish(s, carry):
+        def chips(zz, carry):
+            tok_sib(s, zz).wait_send()
+            h_sib(s, zz).wait_send()
+
+            @pl.when(s > 0)
+            def _():
+                tok_plane(s, zz).wait_send()
+
+            @pl.when((zz <= z) & (z < Z - 1))
+            def _():
+                h_up(s, zz).wait_send()
+
+            @pl.when((zz >= z) & (z > 0))
+            def _():
+                h_dn(s, zz).wait_send()
+
+            return carry
+
+        return lax.fori_loop(0, Z, chips, carry)
+
+    lax.fori_loop(0, E, finish, 0)
+
+
+def gather(tokens, meta, gate_weight, up_weight, E, B):
+    rows, F = tokens.shape
+    D, W = gate_weight.shape[1:]
+    Z = B // 2
+    in_hbm = pl.BlockSpec(memory_space=pltpu.HBM)
+    in_vmem = pl.BlockSpec(memory_space=pltpu.VMEM)
+    dma = pltpu.SemaphoreType.DMA
     return pl.pallas_call(
-        functools.partial(moment_kernel, E),
-        grid_spec=pltpu.PrefetchScalarGridSpec(
-            num_scalar_prefetch=1,
-            grid=(FF // tile,),
-            in_specs=[
-                pl.BlockSpec(meta.shape, lambda i, p: (0, 0, 0)),
-                pl.BlockSpec((rows, W), lambda i, p: (0, p[1])),
-                pl.BlockSpec((rows, tile), lambda i, p: (0, i)),
-            ],
-            out_specs=[
-                pl.BlockSpec((1, W, tile), lambda i, p: (0, 0, i)),
-                pl.BlockSpec((CLASSES, W), lambda i, p: (0, 0)),
-            ],
-            scratch_shapes=[pltpu.VMEM((W, rows), jnp.bfloat16), pltpu.VMEM((8, 128), jnp.float32)],
-        ),
-        out_shape=[jax.ShapeDtypeStruct((1, W, FF), jnp.bfloat16), jax.ShapeDtypeStruct((CLASSES, W), jnp.float32)],
-        compiler_params=pltpu.CompilerParams(vmem_limit_bytes=40 * MIB),
-        name="moments",
-    )(place, meta, hidden, hidden)
+        functools.partial(gather_kernel, E, B),
+        out_shape=[pltpu.VMEM((1, W, B * W), jnp.bfloat16), jax.ShapeDtypeStruct((CLASSES, W), jnp.float32)],
+        in_specs=[in_hbm, in_vmem, in_hbm, in_hbm],
+        out_specs=[in_vmem, in_vmem],
+        scratch_shapes=[
+            pltpu.VMEM((E, rows, D), jnp.bfloat16),
+            pltpu.VMEM((D, W), jnp.bfloat16),
+            pltpu.VMEM((D, W), jnp.bfloat16),
+            pltpu.VMEM((E * rows, B * W), jnp.bfloat16),
+            pltpu.VMEM((E,) + meta.shape, jnp.int32),
+            pltpu.VMEM((W, E * rows), jnp.bfloat16),
+            pltpu.VMEM((8, 128), jnp.float32),
+            dma((4,)), dma((Z,)), dma((E, Z)), dma((E, Z)), dma((E, B)), dma((E,)), dma((E,)),
+            dma((E, Z)), dma((E, Z)), dma((E, Z)), dma((E, B)),
+        ],
+        compiler_params=pltpu.CompilerParams(
+            collective_id=0, has_side_effects=True, vmem_limit_bytes=44 * MIB),
+        name="hidden_moments",
+    )(tokens, meta, gate_weight, up_weight)
 
 
 def plain(tokens, routes, labels, gate_weight, up_weight):
@@ -331,9 +344,7 @@
     if B % 2 or F % 128 or W % 256 or rows != 128:
         return plain(tokens, routes, labels, gate_weight, up_weight)
     meta = jnp.concatenate([routes.T, labels[None], jnp.zeros((5, rows), jnp.int32)], axis=0)
-    hidden, meta_all = gather(tokens, meta, gate_weight, up_weight, E, B)
-    place = jnp.stack([lax.axis_index("expert"), lax.axis_index("blk")]).astype(jnp.int32)
-    moment, cross = moments(place, meta_all, hidden, E, B)
+    moment, cross = gather(tokens, meta, gate_weight, up_weight, E, B)
     return moment, cross.T[None]
 
 

time: 126 us -> 112 us (0.89)
  Pallas kernels: 114 us -> 103 us
  local copies, waits for them, and re-layouts: 9.91 us -> 6.87 us
    pallas_call x2 -> x1, Pallas kernels: 114 us -> 103 us  [gather(): pl.pallas_call(functools.partial(gather_kernel, E, B), out_shape=[pltpu.V...]
    unnamed x8 -> x4, local copies, waits for them, and re-layouts: 9.84 us -> 6.8 us
where the time goes in v2:
time: 112 us
  Pallas kernels  103 us (92%)
  local copies, waits for them, and re-layouts  6.87 us (6%)
  other arithmetic  1.36 us (1%)
    pallas_call x1, Pallas kernels, gather(): pl.pallas_call(functools.partial(gather_kernel, E, B), out_shape=[pltpu.V...  103 us
    unnamed x4, local copies, waits for them, and re-layouts  6.8 us

profile of v2, /device:TPU:0, one launch (start us, length us, event | category | flops | bytes accessed | tf_op | source)
XLA Modules:
  0.0 112.2 jit_solution(4121969699259632558)
XLA Ops:
  0.6 0.1 pad.2.clone
  0.7 1.4 %add_add_fusion.meta_ref = s32[8,128]{1,0:T(8,128)} fusion(s32[1,128]{1,0:T(1,128)} %bitcast.7, s32[2,128]{1,0:T(2,128)} %bitcast.6, s32[8]{0:T(128)S(1)} %pad.2.clone), kind=kLoop, calls=%fused_computation | loop fusion | flops 2048 | bytes 5664 | tf_op jit(solution)/shard_map/concatenate | solution.py:346
  2.1 103.3 %hidden_moments.1 = (bf16[1,1024,8192]{2,1,0:T(8,128)(2,1)S(1)}, f32[16,1024]{1,0:T(8,128)}) custom-call(bf16[128,384]{1,0:T(8,128)(2,1)} %t_ref.1, s32[8,128]{1,0:T(8,128)} %add_add_fusion.meta_ref, bf16[1,3072,1024]{2,1,0:T(8,128)(2,1)} %wg_ref.1, bf16[1,3072,1024]{2,1,0:T(8,128)(2,1)} %wu_ref.1), custom_call_target="tpu_custom_call" | custom-call | tf_op jit(solution)/shard_map/hidden_moments/pallas_call | solution.py:301
  105.4 0.0 copy-start
  105.4 6.2 %copy.9 = bf16[1,1024,8192]{2,1,0:T(8,128)(2,1)} copy(bf16[1,1024,8192]{2,1,0:T(8,128)(2,1)S(1)} %get-tuple-element.6) | data formatting | bytes 33554432
  111.5 0.0 copy-done
  111.6 0.6 copy.10
  (1 shorter events, 0.0 us)
Async XLA Ops:
  105.4 6.2 %copy-start = (f32[16,1024]{1,0:T(8,128)S(1)}, f32[16,1024]{1,0:T(8,128)}, u32[]{:S(2)}) copy-start(f32[16,1024]{1,0:T(8,128)} %get-tuple-element.5) | copy-start | bytes 196612

commit v3 on v2

--- a/solution.py
+++ b/solution.py
@@ -12,12 +12,14 @@
 MESH = pl.DeviceIdType.MESH
 
 
-def gather_kernel(E, B, t_ref, meta_ref, wg_ref, wu_ref, moment_ref, cross_ref,
+def gather_kernel(E, B, t_ref, meta_ref, rc_ref, wg_ref, wu_ref, moment_ref, cross_ref,
                   tok, wg, wu, h_ref, m_ref, lhs, scale, loc_sem, tz_s, tsib_s, tpl_s, t_r, m_s, m_r,
-                  hsib_s, hup_s, hdn_s, h_r):
+                  hsib_s, hup_s, hdn_s, h_r,
+                  mk, g_buf, pq, r_buf, fw_s, fw_r, pqup_s, pqdn_s, pq_r, rp_s, wsib_s, w_r):
     Z = B // 2
     rows, F = t_ref.shape
     W = wg_ref.shape[2]
+    V = W // 2
     e, b = lax.axis_index("expert"), lax.axis_index("blk")
     z, c = b // 2, b % 2
     sib = b + 1 - 2 * c
@@ -45,8 +47,15 @@
     def chunk(s, blk):
         return tok.at[s, :, pl.ds(pl.multiple_of(blk * F, 128), F)]
 
+    def part(s, blk, start, width):
+        return h_ref.at[pl.ds(pl.multiple_of(s * rows, rows), rows),
+                        pl.ds(pl.multiple_of(blk * W + start, 128), width)]
+
     def piece(s, blk):
-        return h_ref.at[pl.ds(pl.multiple_of(s * rows, rows), rows), pl.ds(pl.multiple_of(blk * W, 128), W)]
+        return part(s, blk, 0, V)
+
+    def rest(s, blk):
+        return part(s, blk, V, W - V)
 
     def remote(src, dst, send, recv, expert, blk):
         return pltpu.make_async_remote_copy(
@@ -87,6 +96,101 @@
         blk = 2 * zz + c
         return remote(piece(s, blk), piece(s, blk), hsib_s.at[s, zz], h_r.at[s, blk], e, sib)
 
+    def own_sib(s, core):
+        blk = 2 * z + core
+        return remote(part(s, blk, 0, W), part(s, blk, 0, W), hsib_s.at[s, z], h_r.at[s, blk], e, sib)
+
+    def meet(s):
+        return remote(rest(s, b), g_buf.at[e], fw_s.at[s], fw_r.at[e], s, b)
+
+    def pq_up(zz):
+        return remote(pq.at[zz], pq.at[zz], pqup_s.at[zz], pq_r.at[zz], e, b + 2)
+
+    def pq_dn(zz):
+        return remote(pq.at[zz], pq.at[zz], pqdn_s.at[zz], pq_r.at[zz], e, b - 2)
+
+    def deal(k, zz):
+        blk = 2 * zz + c
+        return remote(r_buf.at[zz, k], rest(e, blk), rp_s.at[k, zz], w_r.at[e, blk], lax.rem(e + k, E), b)
+
+    def w_sib(s, zz):
+        blk = 2 * zz + c
+        return remote(rest(s, blk), rest(s, blk), wsib_s.at[s, zz], w_r.at[s, blk], e, sib)
+
+    def w_here(s, blk):
+        remote(rest(s, blk), rest(s, blk), wsib_s.at[s, 0], w_r.at[s, blk], e, sib).wait_recv()
+
+    def pass_on(zz):
+        @pl.when((zz <= z) & (z < Z - 1))
+        def _():
+            pq_up(zz).start()
+
+        @pl.when((zz >= z) & (z > 0))
+        def _():
+            pq_dn(zz).start()
+
+    def pick():
+        for k in range(1, E):
+            other = lax.rem(e + k, E)
+            remote(rest(e, b), g_buf.at[other], fw_s.at[other], fw_r.at[other], other, b).wait_recv()
+
+        def lanes(i, carry):
+            cols = pl.ds(pl.multiple_of(i * 128, 128), 128)
+            mine = h_ref[pl.ds(pl.multiple_of(e * rows, rows), rows),
+                         pl.ds(pl.multiple_of(b * W + V + i * 128, 128), 128)]
+            for top in range(2):
+                total = mine * mk[top, e]
+                for k in range(1, E):
+                    other = lax.rem(e + k, E)
+                    total += g_buf[other, :, cols] * mk[top, other]
+                pq[z, top, :, cols] = total
+            return carry
+
+        lax.fori_loop(0, (W - V) // 128, lanes, 0)
+        pass_on(z)
+
+    def unpick(zz):
+        remote(pq.at[zz], pq.at[zz], pqup_s.at[zz], pq_r.at[zz], e, sib).wait_recv()
+        pass_on(zz)
+        blk = 2 * zz + c
+
+        def lanes(i, carry):
+            cols = pl.ds(pl.multiple_of(i * 128, 128), 128)
+            first, second = pq[zz, 0, :, cols], pq[zz, 1, :, cols]
+            for k in range(E):
+                other = lax.rem(e + k, E)
+                value = first * mk[0, other] + second * mk[1, other]
+                if k:
+                    r_buf[zz, k, :, cols] = value
+                else:
+                    h_ref[pl.ds(pl.multiple_of(e * rows, rows), rows),
+                          pl.ds(pl.multiple_of(blk * W + V + i * 128, 128), 128)] = value
+            return carry
+
+        lax.fori_loop(0, (W - V) // 128, lanes, 0)
+        for k in range(1, E):
+            deal(k, zz).start()
+        w_sib(e, zz).start()
+
+    def dealt(zz):
+        for k in range(1, E):
+            s = lax.rem(e + k, E)
+            w_here(s, 2 * zz + c)
+            w_sib(s, zz).start()
+
+    def both(d, action):
+        @pl.when((d > 0) & (d < Z) & (z - d >= 0))
+        def _():
+            action(z - d)
+
+        @pl.when((d > 0) & (z + d < Z))
+        def _():
+            action(z + d)
+
+    for top in range(2):
+        for k in range(E):
+            mk[top, k] = (rc_ref[top] == k).astype(mk.dtype)
+
     def h_up(s, zz):
         blk = 2 * zz + c
         return remote(piece(s, blk), piece(s, blk), hup_s.at[s, zz], h_r.at[s, blk], e, b + 2)
@@ -152,7 +256,11 @@
         def _():
             h_dn(s, z).start()
 
-        h_sib(s, z).start()
+        own_sib(s, c).start()
+
+        @pl.when(j > 0)
+        def _():
+            meet(s).start()
 
     def forward(s, d):
         @pl.when(z - d >= 0)
@@ -196,20 +304,28 @@
 
         @pl.when(d == 0)
         def _():
+            pick()
             prepare()
-            block(b)
+            block(b, 0, W)
 
         @pl.when(d > 0)
         def _():
-            @pl.when(z - d >= 0)
-            def _():
-                block(2 * (z - d) + c)
-
-            @pl.when(z + d < Z)
-            def _():
-                block(2 * (z + d) + c)
-
-            from_sibling(d - 1)
+            both(d, unpick)
+            both(d - 1, dealt)
+            both(d, lambda zz: block(2 * zz + c, 0, V))
+
+            @pl.when(d == 1)
+            def _():
+                def shard(s, carry):
+                    own_sib(s, 1 - c).wait_recv()
+                    return carry
+
+                lax.fori_loop(0, E, shard, 0)
+                block(2 * z + 1 - c, 0, W)
+
+            both(d - 1, whole_from_sibling)
+            both(d - 1, lambda zz: block(2 * zz + c, V, W))
+            both(d - 2, rest_from_sibling)
 
         return carry
 
@@ -233,36 +349,32 @@
         cross_ref[...] = lax.dot_general(
             one_hot, masked, (((1,), (1,)), ((), ())), preferred_element_type=jnp.float32) * (CLASSES / count)
 
-    def block(blk):
+    def block(blk, start, stop):
         def columns(i, carry):
             cols = pl.ds(pl.multiple_of(blk * W + i * tile, 128), tile)
             acc = jnp.dot(lhs[...], h_ref[:, cols], preferred_element_type=jnp.float32)
             moment_ref[0, :, cols] = (acc * scale[0:1, 0:1]).astype(moment_ref.dtype)
             return carry
 
-        lax.fori_loop(0, W // tile, columns, 0)
-
-    def from_sibling(d):
-        def arrived(zz):
-            blk = 2 * zz + 1 - c
-
-            def shard(s, carry):
-                h_here(s, blk)
-                return carry
-
-            lax.fori_loop(0, E, shard, 0)
-            block(blk)
-
-        @pl.when(z - d >= 0)
-        def _():
-            arrived(z - d)
-
-        @pl.when((d > 0) & (z + d < Z))
-        def _():
-            arrived(z + d)
-
-    lax.fori_loop(0, E + Z - 1, turn, 0)
-    from_sibling(Z - 1)
+        lax.fori_loop(start // tile, stop // tile, columns, 0)
+
+    def whole_from_sibling(zz):
+        def shard(s, carry):
+            h_here(s, 2 * zz + 1 - c)
+            return carry
+
+        lax.fori_loop(0, E, shard, 0)
+        block(2 * zz + 1 - c, 0, V)
+
+    def rest_from_sibling(zz):
+        def shard(s, carry):
+            w_here(s, 2 * zz + 1 - c)
+            return carry
+
+        lax.fori_loop(0, E, shard, 0)
+        block(2 * zz + 1 - c, V, W)
+
+    lax.fori_loop(0, E + Z + 1, turn, 0)
 
     for d in range(1, Z):
         tok_z(d).wait_send()
@@ -270,7 +382,19 @@
     def finish(s, carry):
         def chips(zz, carry):
             tok_sib(s, zz).wait_send()
-            h_sib(s, zz).wait_send()
+
+            @pl.when(zz == z)
+            def _():
+                own_sib(s, c).wait_send()
+
+            @pl.when(zz != z)
+            def _():
+                h_sib(s, zz).wait_send()
+                w_sib(s, zz).wait_send()
+
+            @pl.when((zz != z) & (s > 0))
+            def _():
+                deal(s, zz).wait_send()
 
             @pl.when(s > 0)
             def _():
@@ -289,9 +413,24 @@
         return lax.fori_loop(0, Z, chips, carry)
 
     lax.fori_loop(0, E, finish, 0)
-
-
-def gather(tokens, meta, gate_weight, up_weight, E, B):
+    for k in range(1, E):
+        meet(lax.rem(e + k, E)).wait_send()
+
+    def lines(zz, carry):
+        @pl.when((zz <= z) & (z < Z - 1))
+        def _():
+            pq_up(zz).wait_send()
+
+        @pl.when((zz >= z) & (z > 0))
+        def _():
+            pq_dn(zz).wait_send()
+
+        return carry
+
+    lax.fori_loop(0, Z, lines, 0)
+
+
+def gather(tokens, meta, columns, gate_weight, up_weight, E, B):
     rows, F = tokens.shape
     D, W = gate_weight.shape[1:]
     Z = B // 2
@@ -301,7 +440,7 @@
     return pl.pallas_call(
         functools.partial(gather_kernel, E, B),
         out_shape=[pltpu.VMEM((1, W, B * W), jnp.bfloat16), jax.ShapeDtypeStruct((CLASSES, W), jnp.float32)],
-        in_specs=[in_hbm, in_vmem, in_hbm, in_hbm],
+        in_specs=[in_hbm, in_vmem, in_vmem, in_hbm, in_hbm],
         out_specs=[in_vmem, in_vmem],
         scratch_shapes=[
             pltpu.VMEM((E, rows, D), jnp.bfloat16),
@@ -313,11 +452,16 @@
             pltpu.VMEM((8, 128), jnp.float32),
             dma((4,)), dma((Z,)), dma((E, Z)), dma((E, Z)), dma((E, B)), dma((E,)), dma((E,)),
             dma((E, Z)), dma((E, Z)), dma((E, Z)), dma((E, B)),
+            pltpu.VMEM((2, E, rows, 128), jnp.bfloat16),
+            pltpu.VMEM((E, rows, W // 2), jnp.bfloat16),
+            pltpu.VMEM((Z, 2, rows, W // 2), jnp.bfloat16),
+            pltpu.VMEM((Z, E, rows, W // 2), jnp.bfloat16),
+            dma((E,)), dma((E,)), dma((Z,)), dma((Z,)), dma((Z,)), dma((E, Z)), dma((E, Z)), dma((E, B)),
         ],
         compiler_params=pltpu.CompilerParams(
             collective_id=0, has_side_effects=True, vmem_limit_bytes=44 * MIB),
         name="hidden_moments",
-    )(tokens, meta, gate_weight, up_weight)
+    )(tokens, meta, columns, gate_weight, up_weight)
 
 
 def plain(tokens, routes, labels, gate_weight, up_weight):
@@ -341,10 +485,11 @@
     E, B = lax.axis_size("expert"), lax.axis_size("blk")
     rows, F = tokens.shape
     W = gate_weight.shape[2]
-    if B % 2 or F % 128 or W % 256 or rows != 128:
+    if B % 2 or F % 128 or W % 512 or rows != 128 or routes.shape[1] != 2:
         return plain(tokens, routes, labels, gate_weight, up_weight)
     meta = jnp.concatenate([routes.T, labels[None], jnp.zeros((5, rows), jnp.int32)], axis=0)
-    moment, cross = gather(tokens, meta, gate_weight, up_weight, E, B)
+    columns = jnp.broadcast_to(routes.T[:, :, None], routes.T.shape + (128,))
+    moment, cross = gather(tokens, meta, columns, gate_weight, up_weight, E, B)
     return moment, cross.T[None]
 
 

time: 112 us -> 108 us (0.964)
  Pallas kernels: 103 us -> 97.8 us
  local copies, waits for them, and re-layouts: 6.87 us -> 8.31 us
    pallas_call x1, Pallas kernels: 103 us -> 97.8 us  [gather(): pl.pallas_call(functools.partial(gather_kernel, E, B), out_shape=[pltpu.V...]
    broadcast_in_dim x0 -> x1, local copies, waits for them, and re-layouts: none -> 1.43 us  [shards(): columns = jnp.broadcast_to(routes.T[:, :, None], routes.T.shape + (128,))]
where the time goes in v3:
time: 108 us
  Pallas kernels  97.8 us (91%)
  local copies, waits for them, and re-layouts  8.31 us (8%)
  other arithmetic  1.36 us (1%)
    pallas_call x1, Pallas kernels, gather(): pl.pallas_call(functools.partial(gather_kernel, E, B), out_shape=[pltpu.V...  97.8 us
    unnamed x4, local copies, waits for them, and re-layouts  6.8 us

profile of v3, /device:TPU:0, one launch (start us, length us, event | category | flops | bytes accessed | tf_op | source)
XLA Modules:
  0.0 108.2 jit_solution(4868894026218288433)
XLA Ops:
  0.6 0.1 pad.2.clone
  0.7 1.4 %add_add_fusion.meta_ref = s32[8,128]{1,0:T(8,128)} fusion(s32[1,128]{1,0:T(1,128)} %bitcast.8, s32[2,128]{1,0:T(2,128)} %bitcast.6, s32[8]{0:T(128)S(1)} %pad.2.clone), kind=kLoop, calls=%fused_computation | loop fusion | flops 2048 | bytes 5664 | tf_op jit(solution)/shard_map/concatenate | solution.py:490
  2.1 1.4 %broadcast_in_dim.17.rc_ref = s32[2,128,128]{2,1,0:T(8,128)} broadcast(s32[2,128]{1,0:T(2,128)} %bitcast.7), dimensions={0,1} | broadcast | bytes 132096 | tf_op jit(solution)/shard_map/broadcast_in_dim | solution.py:491
  3.5 97.8 %hidden_moments.1 = (bf16[1,1024,8192]{2,1,0:T(8,128)(2,1)S(1)}, f32[16,1024]{1,0:T(8,128)}) custom-call(bf16[128,384]{1,0:T(8,128)(2,1)} %t_ref.1, s32[8,128]{1,0:T(8,128)} %add_add_fusion.meta_ref, s32[2,128,128]{2,1,0:T(8,128)} %broadcast_in_dim.17.rc_ref, bf16[1,3072,1024]{2,1,0:T(8,128)(2,1)} %wg_ref.1, bf16[1,3072,1024]{2,1,0:T(8,128)(2,1)} %wu_ref.1), custom_call_target="tpu_custom_call" | custom-call | tf_op jit(solution)/shard_map/hidden_moments/pallas_call | solution.py:440
  101.3 0.0 copy-start
  101.4 6.2 %copy.9 = bf16[1,1024,8192]{2,1,0:T(8,128)(2,1)} copy(bf16[1,1024,8192]{2,1,0:T(8,128)(2,1)S(1)} %get-tuple-element.6) | data formatting | bytes 33554432
  107.5 0.0 copy-done
  107.5 0.6 copy.10
  (1 shorter events, 0.0 us)
Async XLA Ops:
  101.3 6.2 %copy-start = (f32[16,1024]{1,0:T(8,128)S(1)}, f32[16,1024]{1,0:T(8,128)}, u32[]{:S(2)}) copy-start(f32[16,1024]{1,0:T(8,128)} %get-tuple-element.5) | copy-start | bytes 196612

commit v4 on v3

--- a/solution.py
+++ b/solution.py
@@ -24,6 +24,11 @@
     z, c = b // 2, b % 2
     sib = b + 1 - 2 * c
 
+    def mate(k):
+        if E == 4:
+            return 2 * lax.rem(e // 2 + k // 2, 2) + lax.rem(e % 2 + k % 2, 2)
+        return lax.rem(e + k, E)
+
     g_copy = pltpu.make_async_copy(wg_ref.at[0], wg, loc_sem.at[0])
     u_copy = pltpu.make_async_copy(wu_ref.at[0], wu, loc_sem.at[1])
     g_copy.start()
@@ -41,7 +46,7 @@
     for d in range(1, Z):
         greet(e, 2 * lax.rem(z + d, Z) + c)
     for k in range(1, E):
-        greet(lax.rem(e + k, E), b)
+        greet(mate(k), b)
     pl.semaphore_wait(barrier, Z + E - 1)
 
     def chunk(s, blk):
@@ -72,20 +77,20 @@
     def tok_plane(k, zz, src=None):
         blk = 2 * zz + c
         return remote(chunk(e, blk) if src is None else src, chunk(e, blk), tpl_s.at[k, zz], t_r.at[e, blk],
-                      lax.rem(e + k, E), b)
+                      mate(k), b)
 
     def tok_here(s, blk):
         remote(chunk(s, blk), chunk(s, blk), tz_s.at[0], t_r.at[s, blk], e, sib).wait_recv()
 
     def meta_to(k):
-        return remote(meta_ref, m_ref.at[e], m_s.at[k], m_r.at[e], lax.rem(e + k, E), b)
+        return remote(meta_ref, m_ref.at[e], m_s.at[k], m_r.at[e], mate(k), b)
 
     t_copy = pltpu.make_async_copy(t_ref, chunk(e, b), loc_sem.at[2])
     m_copy = pltpu.make_async_copy(meta_ref, m_ref.at[e], loc_sem.at[3])
     for d in range(1, Z):
         tok_z(d).start()
     tok_sib(e, z, t_ref).start()
-    for k in range(1, E):
+    for k in range(1, E - 1):
         tok_plane(k, z, t_ref).start()
     t_copy.start()
     m_copy.start()
@@ -111,7 +116,7 @@
 
     def deal(k, zz):
         blk = 2 * zz + c
-        return remote(r_buf.at[zz, k], rest(e, blk), rp_s.at[k, zz], w_r.at[e, blk], lax.rem(e + k, E), b)
+        return remote(r_buf.at[zz, k], rest(e, blk), rp_s.at[k, zz], w_r.at[e, blk], mate(k), b)
 
     def w_sib(s, zz):
         blk = 2 * zz + c
@@ -131,7 +136,7 @@
 
     def pick():
         for k in range(1, E):
-            other = lax.rem(e + k, E)
+            other = mate(k)
             remote(rest(e, b), g_buf.at[other], fw_s.at[other], fw_r.at[other], other, b).wait_recv()
 
         def lanes(i, carry):
@@ -141,7 +146,7 @@
             for top in range(2):
                 total = mine * mk[top, e]
                 for k in range(1, E):
-                    other = lax.rem(e + k, E)
+                    other = mate(k)
                     total += g_buf[other, :, cols] * mk[top, other]
                 pq[z, top, :, cols] = total
             return carry
@@ -158,7 +163,7 @@
             cols = pl.ds(pl.multiple_of(i * 128, 128), 128)
             first, second = pq[zz, 0, :, cols], pq[zz, 1, :, cols]
             for k in range(E):
-                other = lax.rem(e + k, E)
+                other = mate(k)
                 value = first * mk[0, other] + second * mk[1, other]
                 if k:
                     r_buf[zz, k, :, cols] = value
@@ -174,7 +179,7 @@
 
     def dealt(zz):
         for k in range(1, E):
-            s = lax.rem(e + k, E)
+            s = mate(k)
             w_here(s, 2 * zz + c)
             w_sib(s, zz).start()
 
@@ -211,12 +216,18 @@
                 zz = lax.rem(z + d, Z)
                 tok_here(e, 2 * zz + c)
                 tok_sib(e, zz).start()
-                for k in range(1, E):
+                for k in range(1, E - 1):
                     tok_plane(k, zz).start()
                 return carry
 
             lax.fori_loop(1, Z, arrived, 0)
             t_copy.wait()
+
+            def across(zz, carry):
+                tok_plane(E - 1, zz).start()
+                return carry
+
+            lax.fori_loop(0, Z, across, 0)
             g_copy.wait()
             u_copy.wait()
 
@@ -286,7 +297,7 @@
     def turn(k, carry):
         def inner(i, carry):
             j = E - 1 - i
-            s = lax.rem(e + j, E)
+            s = mate(j)
             d = k - j
 
             @pl.when(d == 0)
@@ -333,7 +344,7 @@
         m_copy.wait()
         for k in range(1, E):
             meta_to(k).wait_send()
-            other = lax.rem(e + k, E)
+            other = mate(k)
             remote(meta_ref, m_ref.at[other], m_s.at[k], m_r.at[other], other, b).wait_recv()
 
         def row(i):
@@ -414,7 +425,7 @@
 
     lax.fori_loop(0, E, finish, 0)
     for k in range(1, E):
-        meet(lax.rem(e + k, E)).wait_send()
+        meet(mate(k)).wait_send()
 
     def lines(zz, carry):
         @pl.when((zz <= z) & (z < Z - 1))

time: 108 us -> 103 us (0.954)
  Pallas kernels: 97.8 us -> 92.6 us
    pallas_call x1, Pallas kernels: 97.8 us -> 92.6 us  [gather(): pl.pallas_call(functools.partial(gather_kernel, E, B), out_shape=[pltpu.V...]
where the time goes in v4:
time: 103 us
  Pallas kernels  92.6 us (90%)
  local copies, waits for them, and re-layouts  8.31 us (8%)
  other arithmetic  1.36 us (1%)
    pallas_call x1, Pallas kernels, gather(): pl.pallas_call(functools.partial(gather_kernel, E, B), out_shape=[pltpu.V...  92.6 us
    unnamed x4, local copies, waits for them, and re-layouts  6.8 us

profile of v4, /device:TPU:0, one launch (start us, length us, event | category | flops | bytes accessed | tf_op | source)
XLA Modules:
  0.0 102.9 jit_solution(15981812448905171089)
XLA Ops:
  0.6 0.1 pad.2.clone
  0.7 1.4 %add_add_fusion.meta_ref = s32[8,128]{1,0:T(8,128)} fusion(s32[1,128]{1,0:T(1,128)} %bitcast.8, s32[2,128]{1,0:T(2,128)} %bitcast.6, s32[8]{0:T(128)S(1)} %pad.2.clone), kind=kLoop, calls=%fused_computation | loop fusion | flops 2048 | bytes 5664 | tf_op jit(solution)/shard_map/concatenate | solution.py:501
  2.1 1.4 %broadcast_in_dim.17.rc_ref = s32[2,128,128]{2,1,0:T(8,128)} broadcast(s32[2,128]{1,0:T(2,128)} %bitcast.7), dimensions={0,1} | broadcast | bytes 132096 | tf_op jit(solution)/shard_map/broadcast_in_dim | solution.py:502
  3.5 92.6 %hidden_moments.1 = (bf16[1,1024,8192]{2,1,0:T(8,128)(2,1)S(1)}, f32[16,1024]{1,0:T(8,128)}) custom-call(bf16[128,384]{1,0:T(8,128)(2,1)} %t_ref.1, s32[8,128]{1,0:T(8,128)} %add_add_fusion.meta_ref, s32[2,128,128]{2,1,0:T(8,128)} %broadcast_in_dim.17.rc_ref, bf16[1,3072,1024]{2,1,0:T(8,128)(2,1)} %wg_ref.1, bf16[1,3072,1024]{2,1,0:T(8,128)(2,1)} %wu_ref.1), custom_call_target="tpu_custom_call" | custom-call | tf_op jit(solution)/shard_map/hidden_moments/pallas_call | solution.py:451
  96.1 0.0 copy-start
  96.1 6.2 %copy.9 = bf16[1,1024,8192]{2,1,0:T(8,128)(2,1)} copy(bf16[1,1024,8192]{2,1,0:T(8,128)(2,1)S(1)} %get-tuple-element.6) | data formatting | bytes 33554432
  102.3 0.0 copy-done
  102.3 0.6 copy.10
  (1 shorter events, 0.0 us)
Async XLA Ops:
  96.1 6.2 %copy-start = (f32[16,1024]{1,0:T(8,128)S(1)}, f32[16,1024]{1,0:T(8,128)}, u32[]{:S(2)}) copy-start(f32[16,1024]{1,0:T(8,128)} %get-tuple-element.5) | copy-start | bytes 196612

commit v5 on v4

--- a/solution.py
+++ b/solution.py
@@ -19,7 +19,7 @@
     Z = B // 2
     rows, F = t_ref.shape
     W = wg_ref.shape[2]
-    V = W // 2
+    V = W // 4
     e, b = lax.axis_index("expert"), lax.axis_index("blk")
     z, c = b // 2, b % 2
     sib = b + 1 - 2 * c
@@ -464,9 +464,9 @@
             dma((4,)), dma((Z,)), dma((E, Z)), dma((E, Z)), dma((E, B)), dma((E,)), dma((E,)),
             dma((E, Z)), dma((E, Z)), dma((E, Z)), dma((E, B)),
             pltpu.VMEM((2, E, rows, 128), jnp.bfloat16),
-            pltpu.VMEM((E, rows, W // 2), jnp.bfloat16),
-            pltpu.VMEM((Z, 2, rows, W // 2), jnp.bfloat16),
-            pltpu.VMEM((Z, E, rows, W // 2), jnp.bfloat16),
+            pltpu.VMEM((E, rows, W - W // 4), jnp.bfloat16),
+            pltpu.VMEM((Z, 2, rows, W - W // 4), jnp.bfloat16),
+            pltpu.VMEM((Z, E, rows, W - W // 4), jnp.bfloat16),
             dma((E,)), dma((E,)), dma((Z,)), dma((Z,)), dma((Z,)), dma((E, Z)), dma((E, Z)), dma((E, B)),
         ],
         compiler_params=pltpu.CompilerParams(
@@ -496,7 +496,7 @@
     E, B = lax.axis_size("expert"), lax.axis_size("blk")
     rows, F = tokens.shape
     W = gate_weight.shape[2]
-    if B % 2 or F % 128 or W % 512 or rows != 128 or routes.shape[1] != 2:
+    if B % 2 or F % 128 or W % 1024 or rows != 128 or routes.shape[1] != 2:
         return plain(tokens, routes, labels, gate_weight, up_weight)
     meta = jnp.concatenate([routes.T, labels[None], jnp.zeros((5, rows), jnp.int32)], axis=0)
     columns = jnp.broadcast_to(routes.T[:, :, None], routes.T.shape + (128,))

time: 103 us -> 107 us (1.039)
  Pallas kernels: 92.6 us -> 96.3 us
    pallas_call x1, Pallas kernels: 92.6 us -> 96.3 us  [gather(): pl.pallas_call(functools.partial(gather_kernel, E, B), out_shape=[pltpu.V...]
where the time goes in v5:
time: 107 us
  Pallas kernels  96.3 us (90%)
  local copies, waits for them, and re-layouts  8.31 us (8%)
  other arithmetic  1.36 us (1%)
    pallas_call x1, Pallas kernels, gather(): pl.pallas_call(functools.partial(gather_kernel, E, B), out_shape=[pltpu.V...  96.3 us
    unnamed x4, local copies, waits for them, and re-layouts  6.8 us

profile of v5, /device:TPU:0, one launch (start us, length us, event | category | flops | bytes accessed | tf_op | source)
XLA Modules:
  0.0 106.6 jit_solution(9829877454707449356)
XLA Ops:
  0.6 0.1 pad.2.clone
  0.7 1.4 %add_add_fusion.meta_ref = s32[8,128]{1,0:T(8,128)} fusion(s32[1,128]{1,0:T(1,128)} %bitcast.8, s32[2,128]{1,0:T(2,128)} %bitcast.6, s32[8]{0:T(128)S(1)} %pad.2.clone), kind=kLoop, calls=%fused_computation | loop fusion | flops 2048 | bytes 5664 | tf_op jit(solution)/shard_map/concatenate | solution.py:501
  2.1 1.4 %broadcast_in_dim.17.rc_ref = s32[2,128,128]{2,1,0:T(8,128)} broadcast(s32[2,128]{1,0:T(2,128)} %bitcast.7), dimensions={0,1} | broadcast | bytes 132096 | tf_op jit(solution)/shard_map/broadcast_in_dim | solution.py:502
  3.5 96.3 %hidden_moments.1 = (bf16[1,1024,8192]{2,1,0:T(8,128)(2,1)S(1)}, f32[16,1024]{1,0:T(8,128)}) custom-call(bf16[128,384]{1,0:T(8,128)(2,1)} %t_ref.1, s32[8,128]{1,0:T(8,128)} %add_add_fusion.meta_ref, s32[2,128,128]{2,1,0:T(8,128)} %broadcast_in_dim.17.rc_ref, bf16[1,3072,1024]{2,1,0:T(8,128)(2,1)} %wg_ref.1, bf16[1,3072,1024]{2,1,0:T(8,128)(2,1)} %wu_ref.1), custom_call_target="tpu_custom_call" | custom-call | tf_op jit(solution)/shard_map/hidden_moments/pallas_call | solution.py:451
  99.8 0.0 copy-start
  99.8 6.2 %copy.9 = bf16[1,1024,8192]{2,1,0:T(8,128)(2,1)} copy(bf16[1,1024,8192]{2,1,0:T(8,128)(2,1)S(1)} %get-tuple-element.6) | data formatting | bytes 33554432
  106.0 0.0 copy-done
  106.0 0.6 copy.10
  (1 shorter events, 0.0 us)
Async XLA Ops:
  99.8 6.2 %copy-start = (f32[16,1024]{1,0:T(8,128)S(1)}, f32[16,1024]{1,0:T(8,128)}, u32[]{:S(2)}) copy-start(f32[16,1024]{1,0:T(8,128)} %get-tuple-element.5) | copy-start | bytes 196612
